TPU v7x, 128 devices: a whole 4x4x4 slice. The times are simulated.
128 devices in a mesh: shard: 16 (over z, x), rep: 8 (over y, core).
Axes of the slice: x: 4, y: 4, z: 4, core: 2. Of those that a mesh axis runs over, the one named last changes fastest.
Arguments:
- gradients: bfloat16 [8, 2048, 59392], P('rep', None, 'shard'), may hold values from -250 to 250
- keep_rows: int32 [8, 16, 464, 32], P('rep', None, 'shard'), may hold values from 0 to 127, as said below
- keep_counts: int32 [8, 16, 464], P('rep', None, 'shard'), may hold values from 16 to 32, as said below
- momentum: float32 [16, 128, 59392], P('rep', 'shard'), may hold values from -3 to 3
Outputs:
- new_momentum: float32 [16, 128, 59392], P('rep', 'shard')
Inputs may be any that keep to these rules, and one draw needn't show every extreme that they name: In each tile of each replica the first keep_counts entries of keep_rows are distinct; later entries are not used. `keep_counts`: each replica has a tile with exactly 32 kept rows.
All inputs are finite; a program needn't handle non-finite values.
Results may differ from a plain program's by a relative error of at most 0.012.
Values may be sent and summed in bfloat16 or wider, within the bound.
A program may use at most 192 MiB of HBM per device.

v0:
```python
import math

import jax
import jax.numpy as jnp
from jax import lax
from jax.sharding import PartitionSpec as P

TILE = 128
KMAX = 32


def cosine_table(order):
    freq = jnp.arange(order, dtype=jnp.float32)[:, None]
    place = jnp.arange(order, dtype=jnp.float32)[None, :]
    norming = jnp.where(freq == 0, math.sqrt(1.0 / order), math.sqrt(2.0 / order))
    return norming * jnp.cos(math.pi * (2.0 * place + 1.0) * freq / (2.0 * order))


def body(gradients, keep_rows, keep_counts, momentum):
    order = TILE
    kept_most = KMAX
    rep_count = lax.axis_size("rep")
    shard_count = lax.axis_size("shard")
    all_rows = gradients.shape[1]
    row_tiles = all_rows // order
    owned_rows = row_tiles // rep_count
    col_local = gradients.shape[2] // order
    cosine = cosine_table(order)
    cosine_half = cosine.astype(jnp.bfloat16)
    grad_tiles = gradients[0].reshape(row_tiles, order, col_local, order)
    first_pass = jnp.einsum(
        "qicj,vj->qicv", grad_tiles, cosine_half, preferred_element_type=jnp.float32
    ).astype(jnp.bfloat16)
    spectra = jnp.einsum(
        "ui,qicv->qcuv", cosine_half, first_pass, preferred_element_type=jnp.float32
    ).astype(jnp.bfloat16)
    row_ids = keep_rows[0]
    row_counts = keep_counts[0]
    live_slot = jnp.arange(kept_most, dtype=jnp.int32)[None, None, :] < row_counts[:, :, None]
    freq_ids = jnp.arange(order, dtype=jnp.int32)
    hit_table = (row_ids[..., None] == freq_ids) & live_slot[..., None]
    picker = hit_table.astype(jnp.bfloat16)
    picked = jnp.einsum(
        "qcku,qcuv->qckv", picker, spectra, preferred_element_type=jnp.float32
    ).astype(jnp.bfloat16)
    labels = jnp.where(live_slot, row_ids, -1).astype(jnp.bfloat16)
    freq_half = jnp.arange(order, dtype=jnp.float32).astype(jnp.bfloat16)
    blocks_in = lax.all_to_all(picked, "rep", split_axis=0, concat_axis=0, tiled=True)
    labels_in = lax.all_to_all(labels, "rep", split_axis=0, concat_axis=0, tiled=True)
    sources = blocks_in.shape[0] // owned_rows
    placed = (labels_in[..., None] == freq_half).astype(jnp.bfloat16)
    placed = placed.reshape((sources, owned_rows) + placed.shape[1:])
    blocks_in = blocks_in.reshape((sources, owned_rows) + blocks_in.shape[1:])
    summed = jnp.einsum("rqcku,rqckv->qcuv", placed, blocks_in, preferred_element_type=jnp.float32)
    energy = lax.psum(jnp.sum(summed * summed), ("shard", "rep"))
    half_decoded = jnp.einsum(
        "ui,qcuv->qicv", cosine, summed, precision=lax.Precision.HIGHEST
    ).astype(jnp.bfloat16)
    local_update = jnp.einsum(
        "qicv,vj->qicj", half_decoded, cosine_half, preferred_element_type=jnp.float32
    )
    local_update = local_update.reshape(owned_rows, order, col_local * order)
    row_update = lax.all_to_all(
        local_update.astype(jnp.bfloat16), "shard", split_axis=1, concat_axis=2, tiled=True
    ).astype(local_update.dtype)
    clip_limit = math.sqrt(all_rows * col_local * order * shard_count)
    shrink = jnp.minimum(1.0, clip_limit / jnp.sqrt(energy))
    return 0.9 * momentum + shrink * row_update


def solution(mesh):
    return jax.shard_map(
        body,
        mesh=mesh,
        in_specs=(
            P("rep", None, "shard"),
            P("rep", None, "shard", None),
            P("rep", None, "shard"),
            P("rep", "shard", None),
        ),
        out_specs=P("rep", "shard", None),
        check_vma=False,
    )
```

profile of v0, /device:TPU:1, one launch (start us, length us, event | category | flops | bytes accessed | tf_op | source)
XLA Modules:
  0.0 236.8 jit_solution(18237277135189668471)
XLA Ops:
  0.0 1.1 select_convert_fusion
  1.1 0.8 reshape.47
  1.8 6.0 %all-to-all-start = ((bf16[8,2,928]{2,1,0:T(2,128)(2,1)}), bf16[8,2,928]{2,1,0:T(2,128)(2,1)S(1)}, u32[]{:S(2)}, u32[]{:S(2)}) async-start(bf16[8,2,928]{2,1,0:T(2,128)(2,1)} %reshape.47), calls=%async_computation | async-start | bytes 65536 | tf_op jit(solution)/shard_map/all_to_all | solution.py:49
  7.8 0.8 iota_compare_fusion.1
  8.7 1.0 copy.52
  9.7 24.7 %reshape.46 = bf16[16,128,29,128]{3,2,1,0:T(8,128)(2,1)} reshape(bf16[1,2048,3712]{2,1,0:T(8,128)(2,1)} %param.4) | data formatting | bytes 30408704 | tf_op jit(solution)/shard_map/reshape;squeeze | solution.py:30
  34.4 17.8 %fusion.2 = bf16[128,16,128,29]{2,0,3,1:T(8,128)(2,1)} fusion(bf16[16,128,29,128]{3,2,1,0:T(8,128)(2,1)} %reshape.46, f32[128]{0:T(128)S(1)} %get-tuple-element.8, f32[128]{0:T(128)S(1)} %get-tuple-element.7), kind=kOutput, calls=%fused_computation.2 | convolution fusion | flops 1946222592 | bytes 30409728 | tf_op jit(solution)/shard_map/qicj,vj->qicv/dot_general | solution.py:31
  52.2 11.0 %fusion.77 = bf16[16,29,128,128]{3,2,1,0:T(8,128)(2,1)} fusion(bf16[128,16,128,29]{2,0,3,1:T(8,128)(2,1)} %fusion.2, f32[128]{0:T(128)S(1)} %get-tuple-element.8, f32[128]{0:T(128)S(1)} %get-tuple-element.7), kind=kOutput, calls=%fused_computation.5.clone.clone.clone.2 | convolution fusion | flops 1953824768 | bytes 30409728 | tf_op jit(solution)/shard_map/ui,qicv->qcuv/dot_general | solution.py:34
  63.3 11.5 %fusion.21 = bf16[16,29,32,128]{3,2,1,0:T(8,128)(2,1)} fusion(s32[16,29,32]{2,1,0:T(8,128)S(1)} %bitcast.59, pred[16,29,32]{2,1,0:T(8,128)(4,1)S(1)} %iota_compare_fusion.1, bf16[16,29,128,128]{3,2,1,0:T(8,128)(2,1)} %fusion.77), kind=kOutput, calls=%fused_computation.20 | convolution fusion | flops 492240896 | bytes 19079680 | tf_op jit(solution)/shard_map/qcku,qcuv->qckv/dot_general | solution.py:43
  74.7 0.0 all-to-all-done
  74.7 4.8 %all-to-all-start.1 = ((bf16[16,29,32,128]{3,2,1,0:T(8,128)(2,1)}), bf16[16,29,32,128]{3,2,1,0:T(8,128)(2,1)}, u32[]{:S(2)}, u32[]{:S(2)}) async-start(bf16[16,29,32,128]{3,2,1,0:T(8,128)(2,1)} %fusion.21), calls=%async_computation.1 | async-start | bytes 7602176 | tf_op jit(solution)/shard_map/all_to_all | solution.py:48
  79.5 0.1 reshape.48
  79.7 0.1 copy.19
  79.8 44.4 %all-to-all-done.1 = bf16[16,29,32,128]{3,2,1,0:T(8,128)(2,1)} async-done(((bf16[16,29,32,128]{3,2,1,0:T(8,128)(2,1)}), bf16[16,29,32,128]{3,2,1,0:T(8,128)(2,1)}, u32[]{:S(2)}, u32[]{:S(2)}) %all-to-all-start.1) | async-done | bytes 3801120 | tf_op jit(solution)/shard_map/all_to_all | solution.py:48
  124.2 7.6 %fusion.17 = (f32[]{:T(128)}, f32[2,29,128,128,1]{3,2,4,1,0:T(8,128)S(1)}) fusion(bf16[8,2,29,32,128]{4,3,2,1,0:T(8,128)(2,1)} %bitcast.6, bf16[128]{0:T(256)(128)(2,1)S(1)} %iota_convert_fusion, bf16[8,2,29,32]{3,0,2,1:T(8,128)(2,1)S(1)} %copy.19), kind=kOutput, calls=%fused_computation.14 | convolution fusion | flops 490340352 | bytes 7632132 | tf_op jit(solution)/shard_map/rqcku,rqckv->qcuv/dot_general | solution.py:54
  131.8 6.2 %fusion.15 = bf16[2,29,128,128]{3,2,1,0:T(8,128)(2,1)S(1)} fusion(f32[2,29,128,128,1]{3,2,4,1,0:T(8,128)S(1)} %get-tuple-element.6, f32[128]{0:T(128)S(1)} %get-tuple-element.8, f32[128]{0:T(128)S(1)} %get-tuple-element.7), kind=kOutput, calls=%fused_computation.11 | convolution fusion | flops 1459666944 | bytes 5702656 | tf_op jit(solution)/shard_map/ui,qcuv->qicv/dot_general | solution.py:56
  138.0 0.9 fusion.33
  138.9 4.0 %copy.28 = bf16[2,128,3712]{2,0,1:T(2,128)(2,1)} copy(bf16[2,128,3712]{1,2,0:T(8,128)(2,1)S(1)} %bitcast.58) | data formatting | bytes 3801088 | tf_op jit(solution)/shard_map/convert_element_type | solution.py:64
  142.9 7.6 %all-to-all-start.2 = ((bf16[2,128,3712]{2,0,1:T(2,128)(2,1)}), bf16[2,128,3712]{2,0,1:T(2,128)(2,1)S(1)}, u32[]{:S(2)}, u32[]{:S(2)}) async-start(bf16[2,128,3712]{2,0,1:T(2,128)(2,1)} %copy.28), calls=%async_computation.2 | async-start | bytes 3801088 | tf_op jit(solution)/shard_map/all_to_all | solution.py:63
  150.5 81.2 %psum.7 = f32[]{:T(128)} all-reduce(f32[]{:T(128)} %get-tuple-element.5), channel_id=1, replica_groups=mesh['shard'=16,'rep'=8] {'shard','rep'}, use_global_device_ids=true, to_apply=%region_1.2 | all-reduce | flops 1 | bytes 8 | tf_op jit(solution)/shard_map/psum | solution.py:55
  232.4 0.0 copy-start
  232.4 0.2 convert_multiply_fusion
  232.7 1.8 copy-done
  234.5 2.3 multiply_add_fusion
  (3 shorter events, 0.0 us)
Async XLA Ops:
  1.8 72.9 %all-to-all-start = ((bf16[8,2,928]{2,1,0:T(2,128)(2,1)}), bf16[8,2,928]{2,1,0:T(2,128)(2,1)S(1)}, u32[]{:S(2)}, u32[]{:S(2)}) async-start(bf16[8,2,928]{2,1,0:T(2,128)(2,1)} %reshape.47), calls=%async_computation | async-start | bytes 65536 | tf_op jit(solution)/shard_map/all_to_all | solution.py:49
  74.7 49.5 %all-to-all-start.1 = ((bf16[16,29,32,128]{3,2,1,0:T(8,128)(2,1)}), bf16[16,29,32,128]{3,2,1,0:T(8,128)(2,1)}, u32[]{:S(2)}, u32[]{:S(2)}) async-start(bf16[16,29,32,128]{3,2,1,0:T(8,128)(2,1)} %fusion.21), calls=%async_computation.1 | async-start | bytes 7602176 | tf_op jit(solution)/shard_map/all_to_all | solution.py:48
  142.9 89.5 %all-to-all-start.2 = ((bf16[2,128,3712]{2,0,1:T(2,128)(2,1)}), bf16[2,128,3712]{2,0,1:T(2,128)(2,1)S(1)}, u32[]{:S(2)}, u32[]{:S(2)}) async-start(bf16[2,128,3712]{2,0,1:T(2,128)(2,1)} %copy.28), calls=%async_computation.2 | async-start | bytes 3801088 | tf_op jit(solution)/shard_map/all_to_all | solution.py:63
  232.4 2.1 copy-start
where the time goes:
time: 238 us; the launch traced here: 237 us
  blocking collectives  81.2 us (34%)
  matrix products  55 us (23%)
  waiting for transfers between devices  44.5 us (19%)
  local copies, waits for them, and re-layouts  32.5 us (14%)
  starting transfers between devices  18.4 us (8%)
  other arithmetic  4.46 us (2%)
    psum x1, blocking collectives, body(): energy = lax.psum(jnp.sum(summed * summed), ('shard', 'rep'))  81.2 us
    all_to_all x1, waiting for transfers between devices, body(): lax.all_to_all(picked, 'rep', split_axis=0, concat_axis=0, tiled=True)  44.4 us
    another operation x1, local copies, waits for them, and re-layouts, body(): grad_tiles = gradients[0].reshape(row_tiles, order, col_local, order)  24.7 us
    dot_general x1, matrix products, body(): jnp.einsum('qicj,vj->qicv', grad_tiles, cosine_half, preferred_element_ty...  17.8 us
    dot_general x1, matrix products, body(): jnp.einsum('qcku,qcuv->qckv', picker, spectra, preferred_element_type=jnp...  11.5 us
    dot_general x1, matrix products, body(): jnp.einsum('ui,qicv->qcuv', cosine_half, first_pass, preferred_element_ty...  11 us
    all_to_all x1, starting transfers between devices, body(): lax.all_to_all(local_update.astype(jnp.bfloat16), 'shard', split_axis=1,...  7.59 us
    dot_general x1, matrix products, body(): jnp.einsum('rqcku,rqckv->qcuv', placed, blocks_in, preferred_element_type...  7.55 us
  transfers between devices with their start and end apart: 3, of which 1 were waited for; matrix products, arithmetic and copies ran while one was open for 28% of the time, Pallas kernels for 0%

commit v1 on v0

v1 whole, which is shorter than its diff:
```python
import functools
import math

import jax
import jax.numpy as jnp
import numpy as np
from jax import lax
from jax.experimental import pallas as pl
from jax.experimental.pallas import tpu as pltpu
from jax.sharding import PartitionSpec as P

TILE = 128
KMAX = 32
REPS = 8
SHARDS = 16
ROW_TILES = 16
OWNED = ROW_TILES // REPS
CHUNKS = (1, 4, 4, 4, 4, 4, 4, 3, 1)
AHEAD = 2
MESH = pl.DeviceIdType.MESH


def cosine_table():
    freq = np.arange(TILE, dtype=np.float64)[:, None]
    place = np.arange(TILE, dtype=np.float64)[None, :]
    norming = np.where(freq == 0, math.sqrt(1.0 / TILE), math.sqrt(2.0 / TILE))
    return norming * np.cos(math.pi * (2.0 * place + 1.0) * freq / (2.0 * TILE))


def dot(a, b, dims=((1,), (0,))):
    return lax.dot_general(a, b, (dims, ((), ())), preferred_element_type=jnp.float32)


def exchange_kernel(
    cols, grads, labels, table, table_t, update, energy_out,
    x_buf, send_buf, recv_buf, upd_buf, lab_mine, lab_send, lab_recv, lab_own, energy,
    energy_a, energy_b,
    x_sem, blk_recv, blk_send, lab_sem, upd_sem, en_sem,
):
    shard = lax.axis_index("shard")
    rep = lax.axis_index("rep")
    starts = [sum(CHUNKS[:k]) for k in range(len(CHUNKS))]
    rep_peers = [lax.rem(rep + j, REPS) for j in range(1, REPS)]
    shard_peers = [lax.rem(shard + j, SHARDS) for j in range(1, SHARDS)]

    def x_copy(k):
        span = pl.ds(starts[k] * TILE, CHUNKS[k] * TILE)
        return pltpu.make_async_copy(grads.at[:, span], x_buf.at[:, span], x_sem.at[k])

    for k in range(len(CHUNKS)):
        x_copy(k).start()

    barrier = pltpu.get_barrier_semaphore()
    for peer in rep_peers:
        pl.semaphore_signal(barrier, inc=1, device_id=(shard, peer), device_id_type=MESH)
    for peer in shard_peers:
        pl.semaphore_signal(barrier, inc=1, device_id=(peer, rep), device_id_type=MESH)

    lab_mine[...] = jnp.zeros_like(lab_mine)
    for group in range(4):
        row = jnp.concatenate([labels[4 * group + t] for t in range(4)], axis=1)
        lab_mine[group, 0:cols] = row
        lab_send[group] = lab_mine[group].astype(jnp.bfloat16)
    energy[...] = jnp.zeros_like(energy)

    pl.semaphore_wait(barrier, REPS + SHARDS - 2)

    def lab_copy(peer):
        return pltpu.make_async_remote_copy(
            src_ref=lab_send.at[peer // 2], dst_ref=lab_recv.at[rep],
            send_sem=lab_sem.at[0], recv_sem=lab_sem.at[1],
            device_id=(shard, peer), device_id_type=MESH)

    for peer in rep_peers:
        lab_copy(peer).start()
    pltpu.make_async_copy(lab_send.at[rep // 2], lab_recv.at[rep], lab_sem.at[1]).start()

    freq = lax.broadcasted_iota(jnp.int32, (TILE, TILE), 0) + 1

    def hits(row):
        return jnp.where(freq == row, 1.0, 0.0).astype(jnp.bfloat16)

    def encode(k):
        x_copy(k).wait()

        def column(c, carry):
            span = pl.ds(pl.multiple_of(c * TILE, TILE), TILE)
            for group in range(4):
                row = lab_mine[group, pl.ds(c, 1), :]
                left = dot(hits(row), table[...], ((0,), (0,))).astype(jnp.bfloat16)
                parts = []
                for t in range(4):
                    q = 4 * group + t
                    tile = x_buf[q * TILE:(q + 1) * TILE, span]
                    parts.append(dot(left[t * KMAX:(t + 1) * KMAX], tile))
                half = jnp.concatenate(parts, axis=0).astype(jnp.bfloat16)
                kept = dot(half, table_t[...]).astype(jnp.bfloat16)
                send_buf[2 * group, c] = kept[:2 * KMAX]
                send_buf[2 * group + 1, c] = kept[2 * KMAX:]
            return carry

        lax.fori_loop(starts[k], starts[k] + CHUNKS[k], column, 0)

    def send_blocks(k):
        span = pl.ds(starts[k], CHUNKS[k])
        for peer in rep_peers:
            pltpu.make_async_remote_copy(
                src_ref=send_buf.at[peer, span], dst_ref=recv_buf.at[rep, span],
                send_sem=blk_send.at[0], recv_sem=blk_recv.at[k],
                device_id=(shard, peer), device_id_type=MESH).start()
        pltpu.make_async_copy(send_buf.at[rep, span], recv_buf.at[rep, span], blk_recv.at[k]).start()

    def own_labels():
        pltpu.make_async_copy(lab_recv, lab_recv, lab_sem.at[1]).wait()
        slot = lax.broadcasted_iota(jnp.int32, lab_send.shape[1:], 1) // KMAX
        for q in range(OWNED):
            for half in range(2):
                total = jnp.zeros(lab_send.shape[1:], jnp.float32)
                for i in range(4):
                    got = lab_recv[4 * half + i].astype(jnp.float32)
                    shift = lax.rem(4 + i - (lax.rem(rep, 2) * 2 + q), 4) * KMAX
                    total += jnp.where(slot == i, pltpu.roll(got, shift, 1), 0.0)
                lab_own[q, half] = total.astype(jnp.int32)

    def decode(k):
        span = pl.ds(starts[k], CHUNKS[k])
        pltpu.make_async_copy(recv_buf.at[:, span], recv_buf.at[:, span], blk_recv.at[k]).wait()

        def column(c, carry):
            outs = []
            for q in range(OWNED):
                places = jnp.concatenate(
                    [hits(lab_own[q, half, pl.ds(c, 1), :]) for half in range(2)], axis=1)
                block = recv_buf[:, c, q * KMAX:(q + 1) * KMAX, :].reshape(REPS * KMAX, TILE)
                summed = dot(places, block)
                energy[...] += jnp.sum((summed * summed).reshape(TILE // 8, 8, TILE), axis=0)
                rows = dot(table_t[...], summed.astype(jnp.bfloat16)).astype(jnp.bfloat16)
                outs.append(dot(rows, table[...]).reshape(SHARDS, TILE // SHARDS, TILE))
            both = jnp.concatenate(outs, axis=1).astype(jnp.bfloat16)
            upd_buf[:, :, pl.ds(pl.multiple_of(c * TILE, TILE), TILE)] = both
            return carry

        lax.fori_loop(starts[k], starts[k] + CHUNKS[k], column, 0)

    def send_update(k):
        width = CHUNKS[k] * TILE
        src = pl.ds(starts[k] * TILE, width)
        dst = pl.ds(pl.multiple_of((shard * cols + starts[k]) * TILE, TILE), width)
        for peer in shard_peers:
            pltpu.make_async_remote_copy(
                src_ref=upd_buf.at[peer, :, src], dst_ref=update.at[:, dst],
                send_sem=upd_sem.at[0], recv_sem=upd_sem.at[1],
                device_id=(peer, rep), device_id_type=MESH).start()
        pltpu.make_async_copy(upd_buf.at[shard, :, src], update.at[:, dst], upd_sem.at[1]).start()

    last = len(CHUNKS)
    for k in range(AHEAD):
        encode(k)
        send_blocks(k)
    own_labels()
    for k in range(last):
        if k + AHEAD < last:
            encode(k + AHEAD)
            send_blocks(k + AHEAD)
        decode(k)
        send_update(k)

    energy_a[shard] = energy[...]
    for peer in shard_peers:
        pltpu.make_async_remote_copy(
            src_ref=energy, dst_ref=energy_a.at[shard],
            send_sem=en_sem.at[0], recv_sem=en_sem.at[1],
            device_id=(peer, rep), device_id_type=MESH).start()
    others = energy_a.at[pl.ds(0, SHARDS - 1)]
    pltpu.make_async_copy(others, others, en_sem.at[1]).wait()
    pltpu.make_async_copy(others, others, en_sem.at[0]).wait()
    energy[...] = jnp.sum(energy_a[...], axis=0)
    energy_b[rep] = energy[...]
    for peer in rep_peers:
        pltpu.make_async_remote_copy(
            src_ref=energy, dst_ref=energy_b.at[rep],
            send_sem=en_sem.at[2], recv_sem=en_sem.at[3],
            device_id=(shard, peer), device_id_type=MESH).start()
    others = energy_b.at[pl.ds(0, REPS - 1)]
    pltpu.make_async_copy(others, others, en_sem.at[3]).wait()
    energy_out[...] = jnp.sum(energy_b[...], axis=0)
    pltpu.make_async_copy(others, others, en_sem.at[2]).wait()

    sent = send_buf.at[pl.ds(0, REPS - 1)]
    pltpu.make_async_copy(sent, sent, blk_send.at[0]).wait()
    sent = lab_recv.at[pl.ds(0, REPS - 1)]
    pltpu.make_async_copy(sent, sent, lab_sem.at[0]).wait()
    sent = upd_buf.at[pl.ds(0, SHARDS - 1)]
    pltpu.make_async_copy(sent, sent, upd_sem.at[0]).wait()
    pltpu.make_async_copy(upd_buf, upd_buf, upd_sem.at[1]).wait()


def step_kernel(limit, momentum, update, energy, out):
    total = jnp.sum(energy[...], keepdims=True)
    shrink = jnp.minimum(1.0, limit / jnp.sqrt(total))
    rows = update[...].astype(jnp.float32).reshape(momentum.shape)
    out[...] = 0.9 * momentum[...] + shrink * rows


def body(gradients, keep_rows, keep_counts, momentum):
    _, all_rows, width = gradients.shape
    cols = width // TILE
    assert sum(CHUNKS) == cols
    cols_pad = -(-cols // 16) * 16
    cosine = cosine_table().astype(np.float32)
    table = jnp.asarray(cosine).astype(jnp.bfloat16)
    table_t = jnp.asarray(np.ascontiguousarray(cosine.T)).astype(jnp.bfloat16)
    live = jnp.arange(KMAX, dtype=jnp.int32) < keep_counts[0][:, :, None]
    labels = jnp.where(live, keep_rows[0] + 1, 0)
    full = SHARDS * width
    vmem = pl.BlockSpec(memory_space=pltpu.VMEM)
    anywhere = pl.BlockSpec(memory_space=pl.ANY)
    block = (REPS, cols, OWNED * KMAX, TILE)
    part = OWNED * TILE // SHARDS
    update, energy = pl.pallas_call(
        functools.partial(exchange_kernel, cols),
        out_shape=(
            jax.ShapeDtypeStruct((part, full), jnp.bfloat16),
            jax.ShapeDtypeStruct((8, TILE), jnp.float32),
        ),
        in_specs=[anywhere, vmem, vmem, vmem],
        out_specs=(anywhere, vmem),
        scratch_shapes=[
            pltpu.VMEM((all_rows, width), jnp.bfloat16),
            pltpu.VMEM(block, jnp.bfloat16),
            pltpu.VMEM(block, jnp.bfloat16),
            pltpu.VMEM((SHARDS, part, width), jnp.bfloat16),
            pltpu.VMEM((4, cols_pad, TILE), jnp.int32),
            pltpu.VMEM((4, cols_pad, TILE), jnp.bfloat16),
            pltpu.VMEM((REPS, cols_pad, TILE), jnp.bfloat16),
            pltpu.VMEM((OWNED, 2, cols_pad, TILE), jnp.int32),
            pltpu.VMEM((8, TILE), jnp.float32),
            pltpu.VMEM((SHARDS, 8, TILE), jnp.float32),
            pltpu.VMEM((REPS, 8, TILE), jnp.float32),
            pltpu.SemaphoreType.DMA((len(CHUNKS),)),
            pltpu.SemaphoreType.DMA((len(CHUNKS),)),
            pltpu.SemaphoreType.DMA((1,)),
            pltpu.SemaphoreType.DMA((2,)),
            pltpu.SemaphoreType.DMA((2,)),
            pltpu.SemaphoreType.DMA((4,)),
        ],
        compiler_params=pltpu.CompilerParams(
            collective_id=0, has_side_effects=True, vmem_limit_bytes=48 * 1024 * 1024),
    )(gradients[0], labels, table, table_t)

    limit = math.sqrt(all_rows * full)
    steps = 8
    wide = full // steps
    return pl.pallas_call(
        functools.partial(step_kernel, limit),
        grid=(steps,),
        out_shape=jax.ShapeDtypeStruct(momentum.shape, momentum.dtype),
        in_specs=[
            pl.BlockSpec((OWNED, part // OWNED, wide), lambda i: (0, 0, i)),
            pl.BlockSpec((part, wide), lambda i: (0, i)),
            pl.BlockSpec((8, TILE), lambda i: (0, 0)),
        ],
        out_specs=pl.BlockSpec((OWNED, part // OWNED, wide), lambda i: (0, 0, i)),
        compiler_params=pltpu.CompilerParams(vmem_limit_bytes=16 * 1024 * 1024),
    )(momentum, update, energy)


def solution(mesh):
    return jax.shard_map(
        body,
        mesh=mesh,
        in_specs=(
            P("rep", None, "shard"),
            P("rep", None, "shard", None),
            P("rep", None, "shard"),
            P("rep", "shard", None),
        ),
        out_specs=P("rep", "shard", None),
        check_vma=False,
    )
```

time: 238 us -> 72.8 us (0.31)
  blocking collectives: 81.2 us -> 0 us
  Pallas kernels: 0 us -> 69.9 us
  matrix products: 55 us -> 0 us
  waiting for transfers between devices: 44.5 us -> 0 us
  local copies, waits for them, and re-layouts: 32.5 us -> 1.51 us
  starting transfers between devices: 18.4 us -> 0 us
  other arithmetic: 4.46 us -> 1.07 us
    psum x1 -> x0, blocking collectives: 81.2 us -> none  [body(): energy = lax.psum(jnp.sum(summed * summed), ('shard', 'rep'))]
    pallas_call x0 -> x2, Pallas kernels: none -> 69.9 us  [the longest x1 65.4 us: body(): pl.pallas_call(functools.partial(exchange_kernel, cols), out_shape=(jax.S...]
    dot_general x6 -> x0, matrix products: 55 us -> none  [the longest x1 17.8 us: body(): jnp.einsum('qicj,vj->qicv', grad_tiles, cosine_half, preferred_element_ty...]
    all_to_all x3 -> x0, waiting for transfers between devices: 44.5 us -> none  [the longest x1 44.4 us: body(): lax.all_to_all(picked, 'rep', split_axis=0, concat_axis=0, tiled=True)]
    another operation x1 -> x0, local copies, waits for them, and re-layouts: 24.7 us -> none  [body(): grad_tiles = gradients[0].reshape(row_tiles, order, col_local, order)]
    all_to_all x3 -> x0, starting transfers between devices: 18.4 us -> none  [the longest x1 7.59 us: body(): lax.all_to_all(local_update.astype(jnp.bfloat16), 'shard', split_axis=1,...]
    convert_element_type x1 -> x0, local copies, waits for them, and re-layouts: 3.96 us -> none  [body(): local_update.astype(jnp.bfloat16)]
  transfers between devices with their start and end apart: 3 -> 0, of which waited for: 1 -> 0; matrix products, arithmetic and copies ran while one was open for 28% -> 0% of each run, Pallas kernels for 0% -> 0%
where the time goes in v1:
time: 72.8 us; the launch traced here: 72.5 us
  Pallas kernels  69.9 us (96%)
  local copies, waits for them, and re-layouts  1.51 us (2%)
  other arithmetic  1.07 us (1%)
    pallas_call x1, Pallas kernels, body(): pl.pallas_call(functools.partial(exchange_kernel, cols), out_shape=(jax.S...  65.4 us
    pallas_call x1, Pallas kernels, body(): pl.pallas_call(functools.partial(step_kernel, limit), grid=(steps,), out_...  4.45 us
    unnamed x6, local copies, waits for them, and re-layouts  1.51 us

profile of v1, /device:TPU:1, one launch (start us, length us, event | category | flops | bytes accessed | tf_op | source)
XLA Modules:
  0.0 72.5 jit_solution(5062503082984747513)
XLA Ops:
  0.0 1.1 %bitcast_select_fusion.labels = s32[16,29,32]{2,1,0:T(8,128)S(1)} fusion(s32[1,16,29,32]{3,1,2,0:T(8,128)} %param.7, s32[16,29]{1,0:T(8,128)} %bitcast.5), kind=kLoop, calls=%fused_computation | loop fusion | flops 44544 | bytes 120640 | tf_op jit(solution)/shard_map/jit(_where)/select_n | solution.py:214
  1.1 0.0 copy-start.1
  1.1 0.7 %copy-done.1 = bf16[128,128]{1,0:T(8,128)(2,1)S(1)} copy-done((bf16[128,128]{1,0:T(8,128)(2,1)S(1)}, bf16[128,128]{1,0:T(8,128)(2,1)}, u32[]{:S(2)}) %copy-start.1) | copy-done | bytes 32792
  1.8 0.0 copy-start.2
  1.8 0.8 %copy-done.2 = bf16[128,128]{1,0:T(8,128)(2,1)S(1)} copy-done((bf16[128,128]{1,0:T(8,128)(2,1)S(1)}, bf16[128,128]{1,0:T(8,128)(2,1)}, u32[]{:S(2)}) %copy-start.2) | copy-done | bytes 32792
  2.6 0.0 copy-start
  2.6 65.4 %shard_map.64 = (bf16[16,59392]{1,0:T(8,128)(2,1)S(1)}, f32[8,128]{1,0:T(8,128)S(1)}) custom-call(bf16[2048,3712]{1,0:T(8,128)(2,1)} %bitcast.4, s32[16,29,32]{2,1,0:T(8,128)S(1)} %bitcast_select_fusion.labels, bf16[128,128]{1,0:T(8,128)(2,1)S(1)} %copy-done.2, bf16[128,128]{1,0:T(8,128)(2,1)S(1)} %copy-done.1), custom_call_target="tpu_custom_call" | custom-call | tf_op jit(solution)/shard_map/pallas_call | solution.py:220
  68.0 0.0 copy-done
  68.1 4.5 %shard_map.65 = f32[2,8,59392]{2,1,0:T(8,128)} custom-call(f32[2,8,59392]{2,1,0:T(8,128)S(1)} %copy-done, bf16[16,59392]{1,0:T(8,128)(2,1)S(1)} %get-tuple-element.7.update, f32[8,128]{1,0:T(8,128)S(1)} %get-tuple-element.8.energy), custom_call_target="tpu_custom_call" | custom-call | tf_op jit(solution)/shard_map/pallas_call | solution.py:254
Async XLA Ops:
  1.1 0.8 %copy-start.1 = (bf16[128,128]{1,0:T(8,128)(2,1)S(1)}, bf16[128,128]{1,0:T(8,128)(2,1)}, u32[]{:S(2)}) copy-start(bf16[128,128]{1,0:T(8,128)(2,1)} %constant.15.table_t) | copy-start | bytes 98308
  1.8 0.8 %copy-start.2 = (bf16[128,128]{1,0:T(8,128)(2,1)S(1)}, bf16[128,128]{1,0:T(8,128)(2,1)}, u32[]{:S(2)}) copy-start(bf16[128,128]{1,0:T(8,128)(2,1)} %constant.14.table) | copy-start | bytes 98308
  2.6 65.4 %copy-start = (f32[2,8,59392]{2,1,0:T(8,128)S(1)}, f32[2,8,59392]{2,1,0:T(8,128)}, u32[]{:S(2)}) copy-start(f32[2,8,59392]{2,1,0:T(8,128)} %momentum.1) | copy-start | bytes 11403268

commit v2 on v1

v2 whole, which is shorter than its diff:
```python
import functools
import math

import jax
import jax.numpy as jnp
import numpy as np
from jax import lax
from jax.experimental import pallas as pl
from jax.experimental.pallas import tpu as pltpu
from jax.sharding import PartitionSpec as P

TILE = 128
KMAX = 32
REPS = 8
SHARDS = 16
ROW_TILES = 16
OWNED = ROW_TILES // REPS
CHUNKS = (1, 2, 4, 4, 4, 4, 4, 4, 2)
AHEAD = 2
EARLY = 1
PAIR = 2
MESH = pl.DeviceIdType.MESH


def cosine_table():
    freq = np.arange(TILE, dtype=np.float64)[:, None]
    place = np.arange(TILE, dtype=np.float64)[None, :]
    norming = np.where(freq == 0, math.sqrt(1.0 / TILE), math.sqrt(2.0 / TILE))
    return norming * np.cos(math.pi * (2.0 * place + 1.0) * freq / (2.0 * TILE))


def dot(a, b, dims=((1,), (0,))):
    return lax.dot_general(a, b, (dims, ((), ())), preferred_element_type=jnp.float32)


def exchange_kernel(
    cols, grads, keep_rows, keep_counts, tables, update, energy_out,
    x_buf, send_buf, recv_buf, upd_buf, rows_buf, counts_buf, tables_buf,
    lab_wide, lab_mine, lab_send, lab_recv, lab_own, energy, energy_row, energy_a, energy_b,
    x_sem, in_sem, blk_recv, blk_send, lab_sem, upd_sem, en_sem, ready,
):
    shard = lax.axis_index("shard")
    rep = lax.axis_index("rep")
    starts = [sum(CHUNKS[:k]) for k in range(len(CHUNKS))]
    rep_peers = [lax.rem(rep // 2 + y, 4) * 2 + lax.rem(rep + core, 2)
                 for y in (2, 1, 3, 0) for core in (0, 1) if y or core]
    hops = sorted(((z, x) for z in range(4) for x in range(4) if z or x), key=lambda p: -(2 - abs(p[0] - 2)) - (2 - abs(p[1] - 2)))
    ring = [lax.rem(shard // 4 + z, 4) * 4 + lax.rem(shard + x, 4) for z, x in hops]
    shard_peers = ring
    near = [peer for peer, (z, x) in zip(ring, hops) if not (z and x)]
    along_z = [peer for peer, (z, x) in zip(ring, hops) if not x]

    def x_copy(k):
        span = pl.ds(starts[k] * TILE, CHUNKS[k] * TILE)
        return pltpu.make_async_copy(grads.at[:, span], x_buf.at[:, span], x_sem.at[k])

    small = [
        pltpu.make_async_copy(keep_rows, rows_buf, in_sem.at[0]),
        pltpu.make_async_copy(keep_counts, counts_buf, in_sem.at[1]),
        pltpu.make_async_copy(tables, tables_buf, in_sem.at[2]),
    ]
    barrier = pltpu.get_barrier_semaphore()
    for copy in small:
        copy.start()
    x_copy(0).start()
    for peer in rep_peers:
        pl.semaphore_signal(barrier, inc=1, device_id=(shard, peer), device_id_type=MESH)
    for peer in near:
        pl.semaphore_signal(barrier, inc=1, device_id=(peer, rep), device_id_type=MESH)
    for k in range(1, len(CHUNKS)):
        x_copy(k).start()

    energy[...] = jnp.zeros_like(energy)
    for copy in small:
        copy.wait()
    table = tables_buf.at[0]
    table_t = tables_buf.at[1]

    for c in range(cols):
        live = lax.broadcasted_iota(jnp.int32, (ROW_TILES, KMAX), 1) < counts_buf[:, c:c + 1]
        wide = jnp.where(live, rows_buf[c] + 1, 0)
        lab_wide[c * ROW_TILES:(c + 1) * ROW_TILES] = jnp.concatenate([wide] * 4, axis=1)
    slot = lax.broadcasted_iota(jnp.int32, (cols, TILE), 1) // KMAX
    lab_mine[...] = jnp.zeros_like(lab_mine)
    for group in range(4):
        row = jnp.zeros((cols, TILE), jnp.int32)
        for t in range(4):
            got = lab_wide[pl.ds(4 * group + t, cols, stride=ROW_TILES), :]
            row = jnp.where(slot == t, got, row)
        lab_mine[group, 0:cols] = row
        lab_send[group] = lab_mine[group].astype(jnp.bfloat16)

    def lab_copy(peer):
        return pltpu.make_async_remote_copy(
            src_ref=lab_send.at[peer // 2], dst_ref=lab_recv.at[rep],
            send_sem=lab_sem.at[0], recv_sem=lab_sem.at[1],
            device_id=(shard, peer), device_id_type=MESH)

    freq = lax.broadcasted_iota(jnp.int32, (TILE, TILE), 0) + 1

    def hits(row):
        return jnp.where(freq == row, 1.0, 0.0).astype(jnp.bfloat16)

    def encode(k):
        x_copy(k).wait()
        pair = min(PAIR, CHUNKS[k])

        def columns(step, carry):
            first = starts[k] + step * pair
            span = pl.ds(pl.multiple_of(first * TILE, TILE), pair * TILE)
            picks = [hits(lab_mine[group, pl.ds(first + i, 1), :]) for i in range(pair) for group in range(4)]
            left = dot(jnp.concatenate(picks, axis=1), table[...], ((0,), (0,))).astype(jnp.bfloat16)
            parts = [[None] * ROW_TILES for _ in range(pair)]
            for q in range(ROW_TILES):
                rows = [left[(i * ROW_TILES + q) * KMAX:(i * ROW_TILES + q + 1) * KMAX] for i in range(pair)]
                both = dot(jnp.concatenate(rows, axis=0), x_buf[q * TILE:(q + 1) * TILE, span])
                for i in range(pair):
                    parts[i][q] = both[i * KMAX:(i + 1) * KMAX, i * TILE:(i + 1) * TILE].astype(jnp.bfloat16)
            half = jnp.concatenate(parts[0] + (parts[1] if pair > 1 else []), axis=0)
            kept = dot(half, table_t[...]).astype(jnp.bfloat16)
            for i in range(pair):
                for peer in range(REPS):
                    at = (i * REPS + peer) * OWNED * KMAX
                    send_buf[peer, first + i] = kept[at:at + OWNED * KMAX]
            return carry

        lax.fori_loop(0, CHUNKS[k] // pair, columns, 0)

    def send_blocks(k):
        span = pl.ds(starts[k], CHUNKS[k])
        for peer in rep_peers:
            pltpu.make_async_remote_copy(
                src_ref=send_buf.at[peer, span], dst_ref=recv_buf.at[rep, span],
                send_sem=blk_send.at[0], recv_sem=blk_recv.at[k],
                device_id=(shard, peer), device_id_type=MESH).start()
        pltpu.make_async_copy(send_buf.at[rep, span], recv_buf.at[rep, span], blk_recv.at[k]).start()

    def own_labels():
        pltpu.make_async_copy(lab_recv, lab_recv, lab_sem.at[1]).wait()
        slot = lax.broadcasted_iota(jnp.int32, lab_send.shape[1:], 1) // KMAX
        for q in range(OWNED):
            for half in range(2):
                total = jnp.zeros(lab_send.shape[1:], jnp.float32)
                for i in range(4):
                    got = lab_recv[4 * half + i].astype(jnp.float32)
                    shift = lax.rem(4 + i - (lax.rem(rep, 2) * 2 + q), 4) * KMAX
                    total += jnp.where(slot == i, pltpu.roll(got, shift, 1), 0.0)
                lab_own[q, half] = total.astype(jnp.int32)

    def decode(k):
        span = pl.ds(starts[k], CHUNKS[k])
        pltpu.make_async_copy(recv_buf.at[:, span], recv_buf.at[:, span], blk_recv.at[k]).wait()

        pair = min(PAIR, CHUNKS[k])

        def columns(step, carry):
            first = starts[k] + step * pair
            sums = []
            for i in range(pair):
                for q in range(OWNED):
                    places = jnp.concatenate(
                        [hits(lab_own[q, half, pl.ds(first + i, 1), :]) for half in range(2)], axis=1)
                    block = recv_buf[:, first + i, q * KMAX:(q + 1) * KMAX, :].reshape(REPS * KMAX, TILE)
                    sums.append(dot(places, block))
            squares = sum(jnp.sum((v * v).reshape(TILE // 8, 8, TILE), axis=0) for v in sums)
            energy[...] += squares
            wide = jnp.concatenate([v.astype(jnp.bfloat16) for v in sums], axis=1)
            rows = dot(table_t[...], wide).astype(jnp.bfloat16)
            tall = jnp.concatenate([rows[:, n * TILE:(n + 1) * TILE] for n in range(len(sums))], axis=0)
            done = dot(tall, table[...]).reshape(len(sums), SHARDS, TILE // SHARDS, TILE)
            for i in range(pair):
                both = jnp.concatenate([done[i * OWNED + q] for q in range(OWNED)], axis=1).astype(jnp.bfloat16)
                upd_buf[:, :, pl.ds(pl.multiple_of((first + i) * TILE, TILE), TILE)] = both
            return carry

        lax.fori_loop(0, CHUNKS[k] // pair, columns, 0)

    def send_update(k):
        width = CHUNKS[k] * TILE
        src = pl.ds(starts[k] * TILE, width)
        dst = pl.ds(pl.multiple_of((shard * cols + starts[k]) * TILE, TILE), width)
        for peer in shard_peers:
            pltpu.make_async_remote_copy(
                src_ref=upd_buf.at[peer, :, src], dst_ref=update.at[:, dst],
                send_sem=upd_sem.at[0], recv_sem=upd_sem.at[1],
                device_id=(peer, rep), device_id_type=MESH).start()
        pltpu.make_async_copy(upd_buf.at[shard, :, src], update.at[:, dst], upd_sem.at[1]).start()

    last = len(CHUNKS)
    for k in range(EARLY):
        encode(k)
    pl.semaphore_wait(barrier, REPS - 1 + len(near))
    send_blocks(0)
    for peer in rep_peers:
        lab_copy(peer).start()
    pltpu.make_async_copy(lab_send.at[rep // 2], lab_recv.at[rep], lab_sem.at[1]).start()
    for peer in along_z:
        pl.semaphore_signal(ready, inc=1, device_id=(peer, rep), device_id_type=MESH)
    for k in range(1, EARLY):
        send_blocks(k)
    for k in range(EARLY, AHEAD):
        encode(k)
        send_blocks(k)
    for k in range(last):
        if k + AHEAD < last:
            encode(k + AHEAD)
            send_blocks(k + AHEAD)
        if k == 0:
            own_labels()
        decode(k)
        if k == 0:
            pl.semaphore_wait(ready, len(along_z))
        send_update(k)

    sent = send_buf.at[pl.ds(0, REPS - 1)]
    pltpu.make_async_copy(sent, sent, blk_send.at[0]).wait()
    energy_row[0] = jnp.sum(energy[...], axis=0, keepdims=True)
    energy_a[shard] = energy_row[0]
    for peer in shard_peers:
        pltpu.make_async_remote_copy(
            src_ref=energy_row.at[0], dst_ref=energy_a.at[shard],
            send_sem=en_sem.at[0], recv_sem=en_sem.at[1],
            device_id=(peer, rep), device_id_type=MESH).start()
    sent = lab_recv.at[pl.ds(0, REPS - 1)]
    pltpu.make_async_copy(sent, sent, lab_sem.at[0]).wait()
    others = energy_a.at[pl.ds(0, SHARDS - 1)]
    pltpu.make_async_copy(others, others, en_sem.at[1]).wait()
    energy_row[1] = jnp.sum(energy_a[...], axis=0)
    energy_b[rep] = energy_row[1]
    for peer in rep_peers:
        pltpu.make_async_remote_copy(
            src_ref=energy_row.at[1], dst_ref=energy_b.at[rep],
            send_sem=en_sem.at[2], recv_sem=en_sem.at[3],
            device_id=(shard, peer), device_id_type=MESH).start()
    pltpu.make_async_copy(others, others, en_sem.at[0]).wait()
    sent = upd_buf.at[pl.ds(0, SHARDS - 1)]
    pltpu.make_async_copy(sent, sent, upd_sem.at[0]).wait()
    pltpu.make_async_copy(upd_buf, upd_buf, upd_sem.at[1]).wait()
    others = energy_b.at[pl.ds(0, REPS - 1)]
    pltpu.make_async_copy(others, others, en_sem.at[3]).wait()
    energy_out[...] = jnp.sum(energy_b[...], axis=0)
    pltpu.make_async_copy(others, others, en_sem.at[2]).wait()


def step_kernel(limit, momentum, update, energy, out, out_buf, sems):
    total = jnp.sum(energy[...], keepdims=True)
    shrink = jnp.minimum(1.0, limit / jnp.sqrt(total))
    steps = sems.shape[0]
    wide = momentum.shape[2] // steps
    copies = []
    for i in range(steps):
        span = pl.ds(i * wide, wide)
        rows = update[:, span].astype(jnp.float32)
        for q in range(OWNED):
            height = momentum.shape[1]
            out_buf[q, :, span] = 0.9 * momentum[q, :, span] + shrink * rows[q * height:(q + 1) * height]
        copies.append(pltpu.make_async_copy(out_buf.at[:, :, span], out.at[:, :, span], sems.at[i]))
        copies[-1].start()
    for copy in copies:
        copy.wait()


def body(gradients, keep_rows, keep_counts, momentum):
    _, all_rows, width = gradients.shape
    cols = width // TILE
    assert sum(CHUNKS) == cols
    cols_pad = -(-cols // 16) * 16
    cosine = cosine_table().astype(np.float32)
    tables = jnp.asarray(np.stack([cosine, cosine.T])).astype(jnp.bfloat16)
    full = SHARDS * width
    vmem = pl.BlockSpec(memory_space=pltpu.VMEM)
    anywhere = pl.BlockSpec(memory_space=pl.ANY)
    block = (REPS, cols, OWNED * KMAX, TILE)
    part = OWNED * TILE // SHARDS
    update, energy = pl.pallas_call(
        functools.partial(exchange_kernel, cols),
        out_shape=(
            jax.ShapeDtypeStruct((part, full), jnp.bfloat16),
            jax.ShapeDtypeStruct((1, TILE), jnp.float32),
        ),
        in_specs=[pl.BlockSpec(memory_space=pltpu.HBM)] * 4,
        out_specs=(anywhere, vmem),
        scratch_shapes=[
            pltpu.VMEM((all_rows, width), jnp.bfloat16),
            pltpu.VMEM(block, jnp.bfloat16),
            pltpu.VMEM(block, jnp.bfloat16),
            pltpu.VMEM((SHARDS, part, width), jnp.bfloat16),
            pltpu.VMEM((cols, ROW_TILES, KMAX), jnp.int32),
            pltpu.VMEM((ROW_TILES, cols), jnp.int32),
            pltpu.VMEM((2, TILE, TILE), jnp.bfloat16),
            pltpu.VMEM((cols * ROW_TILES, TILE), jnp.int32),
            pltpu.VMEM((4, cols_pad, TILE), jnp.int32),
            pltpu.VMEM((4, cols_pad, TILE), jnp.bfloat16),
            pltpu.VMEM((REPS, cols_pad, TILE), jnp.bfloat16),
            pltpu.VMEM((OWNED, 2, cols_pad, TILE), jnp.int32),
            pltpu.VMEM((8, TILE), jnp.float32),
            pltpu.VMEM((2, 1, TILE), jnp.float32),
            pltpu.VMEM((SHARDS, 1, TILE), jnp.float32),
            pltpu.VMEM((REPS, 1, TILE), jnp.float32),
            pltpu.SemaphoreType.DMA((len(CHUNKS),)),
            pltpu.SemaphoreType.DMA((3,)),
            pltpu.SemaphoreType.DMA((len(CHUNKS),)),
            pltpu.SemaphoreType.DMA((1,)),
            pltpu.SemaphoreType.DMA((2,)),
            pltpu.SemaphoreType.DMA((2,)),
            pltpu.SemaphoreType.DMA((4,)),
            pltpu.SemaphoreType.REGULAR,
        ],
        compiler_params=pltpu.CompilerParams(
            collective_id=0, has_side_effects=True, vmem_limit_bytes=48 * 1024 * 1024),
    )(gradients[0], jnp.transpose(keep_rows[0], (1, 0, 2)), keep_counts[0], tables)

    limit = math.sqrt(all_rows * full)
    return pl.pallas_call(
        functools.partial(step_kernel, limit),
        out_shape=jax.ShapeDtypeStruct(momentum.shape, momentum.dtype),
        in_specs=[vmem, vmem, vmem],
        out_specs=anywhere,
        scratch_shapes=[pltpu.VMEM(momentum.shape, jnp.float32), pltpu.SemaphoreType.DMA((8,))],
        compiler_params=pltpu.CompilerParams(vmem_limit_bytes=16 * 1024 * 1024),
    )(momentum, update, energy)


def solution(mesh):
    return jax.shard_map(
        body,
        mesh=mesh,
        in_specs=(
            P("rep", None, "shard"),
            P("rep", None, "shard", None),
            P("rep", None, "shard"),
            P("rep", "shard", None),
        ),
        out_specs=P("rep", "shard", None),
        check_vma=False,
    )
```

time: 72.8 us -> 67 us (0.920)
  Pallas kernels: 69.9 us -> 64.2 us
  other arithmetic: 1.07 us -> 0 us
  local copies, waits for them, and re-layouts: 1.51 us -> 2.48 us
    pallas_call x1, Pallas kernels: 65.4 us -> 62.1 us  [body(): pl.pallas_call(functools.partial(exchange_kernel, cols), out_shape=(jax.S...]
    pallas_call x1, Pallas kernels: 4.45 us -> 2.15 us  [body(): pl.pallas_call(functools.partial(step_kernel, limit), out_shape=jax.Shape...]
    select_n x1 -> x0, other arithmetic: 1.07 us -> none  [body(): labels = jnp.where(live, keep_rows[0] + 1, 0)]
    unnamed x6 -> x8, local copies, waits for them, and re-layouts: 1.51 us -> 2.48 us
where the time goes in v2:
time: 67 us; the launch traced here: 66.8 us
  Pallas kernels  64.2 us (96%)
  local copies, waits for them, and re-layouts  2.48 us (4%)
    pallas_call x1, Pallas kernels, body(): pl.pallas_call(functools.partial(exchange_kernel, cols), out_shape=(jax.S...  62.1 us
    unnamed x8, local copies, waits for them, and re-layouts  2.48 us
    pallas_call x1, Pallas kernels, body(): pl.pallas_call(functools.partial(step_kernel, limit), out_shape=jax.Shape...  2.15 us

profile of v2, /device:TPU:1, one launch (start us, length us, event | category | flops | bytes accessed | tf_op | source)
XLA Modules:
  0.0 66.8 jit_solution(1952462677588859667)
XLA Ops:
  0.0 0.0 copy-start.1
  0.0 0.9 %copy-done.1 = s32[1,16,29,32]{3,1,2,0:T(8,128)S(1)} copy-done((s32[1,16,29,32]{3,1,2,0:T(8,128)S(1)}, s32[1,16,29,32]{3,1,2,0:T(8,128)}, u32[]{:S(2)}) %copy-start.1) | copy-done | bytes 59416
  0.9 0.0 copy-start.2
  0.9 0.8 %copy-done.2 = bf16[2,128,128]{2,1,0:T(8,128)(2,1)S(1)} copy-done((bf16[2,128,128]{2,1,0:T(8,128)(2,1)S(1)}, bf16[2,128,128]{2,1,0:T(8,128)(2,1)}, u32[]{:S(2)}) %copy-start.2) | copy-done | bytes 65560
  1.8 0.0 copy-start.3
  1.8 0.7 %copy-done.3 = s32[1,16,29]{2,1,0:T(8,128)S(1)} copy-done((s32[1,16,29]{2,1,0:T(8,128)S(1)}, s32[1,16,29]{2,1,0:T(8,128)}, u32[]{:S(2)}) %copy-start.3) | copy-done | bytes 1880
  2.5 0.0 copy-start
  2.5 62.1 %shard_map.55 = (bf16[16,59392]{1,0:T(8,128)(2,1)S(1)}, f32[1,128]{1,0:T(1,128)S(1)}) custom-call(bf16[2048,3712]{1,0:T(8,128)(2,1)} %bitcast.7, s32[29,16,32]{2,1,0:T(8,128)S(1)} %bitcast.5, s32[16,29]{1,0:T(8,128)S(1)} %bitcast.6, bf16[2,128,128]{2,1,0:T(8,128)(2,1)S(1)} %copy-done.2), custom_call_target="tpu_custom_call" | custom-call | tf_op jit(solution)/shard_map/pallas_call | solution.py:275
  64.6 0.0 copy-done
  64.6 2.1 %shard_map.56 = f32[2,8,59392]{2,1,0:T(8,128)} custom-call(f32[2,8,59392]{2,1,0:T(8,128)S(1)} %copy-done, bf16[16,59392]{1,0:T(8,128)(2,1)S(1)} %get-tuple-element.7.update, f32[1,128]{1,0:T(1,128)S(1)} %get-tuple-element.8.energy), custom_call_target="tpu_custom_call" | custom-call | tf_op jit(solution)/shard_map/pallas_call | solution.py:314
Async XLA Ops:
  0.0 0.9 %copy-start.1 = (s32[1,16,29,32]{3,1,2,0:T(8,128)S(1)}, s32[1,16,29,32]{3,1,2,0:T(8,128)}, u32[]{:S(2)}) copy-start(s32[1,16,29,32]{3,1,2,0:T(8,128)} %param.6) | copy-start | bytes 178180
  0.9 0.8 %copy-start.2 = (bf16[2,128,128]{2,1,0:T(8,128)(2,1)S(1)}, bf16[2,128,128]{2,1,0:T(8,128)(2,1)}, u32[]{:S(2)}) copy-start(bf16[2,128,128]{2,1,0:T(8,128)(2,1)} %constant.7.tables) | copy-start | bytes 196612
  1.8 0.7 %copy-start.3 = (s32[1,16,29]{2,1,0:T(8,128)S(1)}, s32[1,16,29]{2,1,0:T(8,128)}, u32[]{:S(2)}) copy-start(s32[1,16,29]{2,1,0:T(8,128)} %param.7) | copy-start | bytes 5572
  2.5 62.1 %copy-start = (f32[2,8,59392]{2,1,0:T(8,128)S(1)}, f32[2,8,59392]{2,1,0:T(8,128)}, u32[]{:S(2)}) copy-start(f32[2,8,59392]{2,1,0:T(8,128)} %momentum.1) | copy-start | bytes 11403268

commit v3 on v2

--- a/solution.py
+++ b/solution.py
@@ -15,9 +15,8 @@
 SHARDS = 16
 ROW_TILES = 16
 OWNED = ROW_TILES // REPS
-CHUNKS = (1, 2, 4, 4, 4, 4, 4, 4, 2)
-AHEAD = 2
-EARLY = 1
+CHUNKS = (1, 2, 4, 4, 4, 4, 4, 2, 2, 1, 1)
+AHEAD = 3
 PAIR = 2
 MESH = pl.DeviceIdType.MESH
 
@@ -46,7 +45,7 @@
                  for y in (2, 1, 3, 0) for core in (0, 1) if y or core]
     hops = sorted(((z, x) for z in range(4) for x in range(4) if z or x), key=lambda p: -(2 - abs(p[0] - 2)) - (2 - abs(p[1] - 2)))
     ring = [lax.rem(shard // 4 + z, 4) * 4 + lax.rem(shard + x, 4) for z, x in hops]
-    shard_peers = ring
+    shard_peers = [j + (j >= shard).astype(jnp.int32) for j in range(SHARDS - 1)]
     near = [peer for peer, (z, x) in zip(ring, hops) if not (z and x)]
     along_z = [peer for peer, (z, x) in zip(ring, hops) if not x]
 
@@ -60,13 +59,13 @@
         pltpu.make_async_copy(tables, tables_buf, in_sem.at[2]),
     ]
     barrier = pltpu.get_barrier_semaphore()
-    for copy in small:
-        copy.start()
-    x_copy(0).start()
     for peer in rep_peers:
         pl.semaphore_signal(barrier, inc=1, device_id=(shard, peer), device_id_type=MESH)
     for peer in near:
         pl.semaphore_signal(barrier, inc=1, device_id=(peer, rep), device_id_type=MESH)
+    for copy in small:
+        copy.start()
+    x_copy(0).start()
     for k in range(1, len(CHUNKS)):
         x_copy(k).start()
 
@@ -76,23 +75,33 @@
     table = tables_buf.at[0]
     table_t = tables_buf.at[1]
 
-    for c in range(cols):
-        live = lax.broadcasted_iota(jnp.int32, (ROW_TILES, KMAX), 1) < counts_buf[:, c:c + 1]
-        wide = jnp.where(live, rows_buf[c] + 1, 0)
-        lab_wide[c * ROW_TILES:(c + 1) * ROW_TILES] = jnp.concatenate([wide] * 4, axis=1)
-    slot = lax.broadcasted_iota(jnp.int32, (cols, TILE), 1) // KMAX
+    def own_rows(first, count):
+        for c in range(first, first + count):
+            live = lax.broadcasted_iota(jnp.int32, (ROW_TILES, KMAX), 1) < counts_buf[:, c:c + 1]
+            wide = jnp.where(live, rows_buf[c] + 1, 0)
+            lab_wide[c * ROW_TILES:(c + 1) * ROW_TILES] = jnp.concatenate([wide] * 4, axis=1)
+        slot = lax.broadcasted_iota(jnp.int32, (count, TILE), 1) // KMAX
+        for group in range(4):
+            row = jnp.zeros((count, TILE), jnp.int32)
+            for t in range(4):
+                got = lab_wide[pl.ds(first * ROW_TILES + 4 * group + t, count, stride=ROW_TILES), :]
+                row = jnp.where(slot == t, got, row)
+            lab_mine[group, first:first + count] = row
+
+    def pack_rows():
+        half = lab_send.shape[1]
+        lower = lax.broadcasted_iota(jnp.int32, (half, TILE), 1) < TILE // 2
+        for group in range(4):
+            early, late = lab_mine[group, 0:half], lab_mine[group, half:2 * half]
+            lab_send[2 * group] = jnp.where(lower, early, pltpu.roll(late, TILE // 2, 1)).astype(jnp.bfloat16)
+            lab_send[2 * group + 1] = jnp.where(lower, pltpu.roll(early, TILE // 2, 1), late).astype(jnp.bfloat16)
+
     lab_mine[...] = jnp.zeros_like(lab_mine)
-    for group in range(4):
-        row = jnp.zeros((cols, TILE), jnp.int32)
-        for t in range(4):
-            got = lab_wide[pl.ds(4 * group + t, cols, stride=ROW_TILES), :]
-            row = jnp.where(slot == t, got, row)
-        lab_mine[group, 0:cols] = row
-        lab_send[group] = lab_mine[group].astype(jnp.bfloat16)
+    own_rows(0, 1)
 
     def lab_copy(peer):
         return pltpu.make_async_remote_copy(
-            src_ref=lab_send.at[peer // 2], dst_ref=lab_recv.at[rep],
+            src_ref=lab_send.at[peer], dst_ref=lab_recv.at[rep],
             send_sem=lab_sem.at[0], recv_sem=lab_sem.at[1],
             device_id=(shard, peer), device_id_type=MESH)
 
@@ -137,17 +146,20 @@
 
     def own_labels():
         pltpu.make_async_copy(lab_recv, lab_recv, lab_sem.at[1]).wait()
-        slot = lax.broadcasted_iota(jnp.int32, lab_send.shape[1:], 1) // KMAX
-        for q in range(OWNED):
-            for half in range(2):
-                total = jnp.zeros(lab_send.shape[1:], jnp.float32)
-                for i in range(4):
-                    got = lab_recv[4 * half + i].astype(jnp.float32)
-                    shift = lax.rem(4 + i - (lax.rem(rep, 2) * 2 + q), 4) * KMAX
-                    total += jnp.where(slot == i, pltpu.roll(got, shift, 1), 0.0)
-                lab_own[q, half] = total.astype(jnp.int32)
-
-    def decode(k):
+        half = lab_send.shape[1]
+        slot = lax.broadcasted_iota(jnp.int32, (half, TILE), 1) // KMAX
+        for part in range(2):
+            for group in range(2):
+                for q in range(OWNED):
+                    total = jnp.zeros((half, TILE), jnp.float32)
+                    for i in range(4):
+                        got = lab_recv[4 * group + i].astype(jnp.float32)
+                        shift = (i - q - 2 * part) % 4 * KMAX
+                        moved = pltpu.roll(got, shift, 1) if shift else got
+                        total = jnp.where(slot == i, moved, total)
+                    lab_own[q, group, part * half:(part + 1) * half] = total.astype(jnp.int32)
+
+    def decode(k, summed_up=None):
         span = pl.ds(starts[k], CHUNKS[k])
         pltpu.make_async_copy(recv_buf.at[:, span], recv_buf.at[:, span], blk_recv.at[k]).wait()
 
@@ -164,6 +176,8 @@
                     sums.append(dot(places, block))
             squares = sum(jnp.sum((v * v).reshape(TILE // 8, 8, TILE), axis=0) for v in sums)
             energy[...] += squares
+            if summed_up is not None:
+                summed_up()
             wide = jnp.concatenate([v.astype(jnp.bfloat16) for v in sums], axis=1)
             rows = dot(table_t[...], wide).astype(jnp.bfloat16)
             tall = jnp.concatenate([rows[:, n * TILE:(n + 1) * TILE] for n in range(len(sums))], axis=0)
@@ -173,7 +187,10 @@
                 upd_buf[:, :, pl.ds(pl.multiple_of((first + i) * TILE, TILE), TILE)] = both
             return carry
 
-        lax.fori_loop(0, CHUNKS[k] // pair, columns, 0)
+        if CHUNKS[k] == pair:
+            columns(0, 0)
+        else:
+            lax.fori_loop(0, CHUNKS[k] // pair, columns, 0)
 
     def send_update(k):
         width = CHUNKS[k] * TILE
@@ -186,19 +203,29 @@
                 device_id=(peer, rep), device_id_type=MESH).start()
         pltpu.make_async_copy(upd_buf.at[shard, :, src], update.at[:, dst], upd_sem.at[1]).start()
 
+    def send_energy():
+        energy_row[0] = jnp.sum(energy[...], axis=0, keepdims=True)
+        energy_a[shard] = energy_row[0]
+        for peer in shard_peers:
+            pltpu.make_async_remote_copy(
+                src_ref=energy_row.at[0], dst_ref=energy_a.at[shard],
+                send_sem=en_sem.at[0], recv_sem=en_sem.at[1],
+                device_id=(peer, rep), device_id_type=MESH).start()
+
     last = len(CHUNKS)
-    for k in range(EARLY):
-        encode(k)
+    encode(0)
     pl.semaphore_wait(barrier, REPS - 1 + len(near))
     send_blocks(0)
+    own_rows(1, cols - 1)
+    encode(1)
+    send_blocks(1)
+    pack_rows()
     for peer in rep_peers:
         lab_copy(peer).start()
-    pltpu.make_async_copy(lab_send.at[rep // 2], lab_recv.at[rep], lab_sem.at[1]).start()
+    pltpu.make_async_copy(lab_send.at[rep], lab_recv.at[rep], lab_sem.at[1]).start()
     for peer in along_z:
         pl.semaphore_signal(ready, inc=1, device_id=(peer, rep), device_id_type=MESH)
-    for k in range(1, EARLY):
-        send_blocks(k)
-    for k in range(EARLY, AHEAD):
+    for k in range(2, AHEAD):
         encode(k)
         send_blocks(k)
     for k in range(last):
@@ -207,20 +234,13 @@
             send_blocks(k + AHEAD)
         if k == 0:
             own_labels()
-        decode(k)
+        decode(k, send_energy if k == last - 1 else None)
         if k == 0:
             pl.semaphore_wait(ready, len(along_z))
         send_update(k)
 
     sent = send_buf.at[pl.ds(0, REPS - 1)]
     pltpu.make_async_copy(sent, sent, blk_send.at[0]).wait()
-    energy_row[0] = jnp.sum(energy[...], axis=0, keepdims=True)
-    energy_a[shard] = energy_row[0]
-    for peer in shard_peers:
-        pltpu.make_async_remote_copy(
-            src_ref=energy_row.at[0], dst_ref=energy_a.at[shard],
-            send_sem=en_sem.at[0], recv_sem=en_sem.at[1],
-            device_id=(peer, rep), device_id_type=MESH).start()
     sent = lab_recv.at[pl.ds(0, REPS - 1)]
     pltpu.make_async_copy(sent, sent, lab_sem.at[0]).wait()
     others = energy_a.at[pl.ds(0, SHARDS - 1)]
@@ -264,7 +284,7 @@
     _, all_rows, width = gradients.shape
     cols = width // TILE
     assert sum(CHUNKS) == cols
-    cols_pad = -(-cols // 16) * 16
+    cols_pad = -(-cols // 32) * 32
     cosine = cosine_table().astype(np.float32)
     tables = jnp.asarray(np.stack([cosine, cosine.T])).astype(jnp.bfloat16)
     full = SHARDS * width
@@ -290,8 +310,8 @@
             pltpu.VMEM((2, TILE, TILE), jnp.bfloat16),
             pltpu.VMEM((cols * ROW_TILES, TILE), jnp.int32),
             pltpu.VMEM((4, cols_pad, TILE), jnp.int32),
-            pltpu.VMEM((4, cols_pad, TILE), jnp.bfloat16),
-            pltpu.VMEM((REPS, cols_pad, TILE), jnp.bfloat16),
+            pltpu.VMEM((REPS, cols_pad // 2, TILE), jnp.bfloat16),
+            pltpu.VMEM((REPS, cols_pad // 2, TILE), jnp.bfloat16),
             pltpu.VMEM((OWNED, 2, cols_pad, TILE), jnp.int32),
             pltpu.VMEM((8, TILE), jnp.float32),
             pltpu.VMEM((2, 1, TILE), jnp.float32),

time: 67 us -> 65 us (0.970)
  Pallas kernels: 64.2 us -> 62.3 us
    pallas_call x1, Pallas kernels: 62.1 us -> 60.2 us  [body(): pl.pallas_call(functools.partial(exchange_kernel, cols), out_shape=(jax.S...]
where the time goes in v3:
time: 65 us; the launch traced here: 64.8 us
  Pallas kernels  62.3 us (96%)
  local copies, waits for them, and re-layouts  2.48 us (4%)
    pallas_call x1, Pallas kernels, body(): pl.pallas_call(functools.partial(exchange_kernel, cols), out_shape=(jax.S...  60.2 us
    unnamed x8, local copies, waits for them, and re-layouts  2.48 us
    pallas_call x1, Pallas kernels, body(): pl.pallas_call(functools.partial(step_kernel, limit), out_shape=jax.Shape...  2.15 us

profile of v3, /device:TPU:1, one launch (start us, length us, event | category | flops | bytes accessed | tf_op | source)
XLA Modules:
  0.0 64.8 jit_solution(11530836771850562418)
XLA Ops:
  0.0 0.0 copy-start.1
  0.0 0.9 %copy-done.1 = s32[1,16,29,32]{3,1,2,0:T(8,128)S(1)} copy-done((s32[1,16,29,32]{3,1,2,0:T(8,128)S(1)}, s32[1,16,29,32]{3,1,2,0:T(8,128)}, u32[]{:S(2)}) %copy-start.1) | copy-done | bytes 59416
  0.9 0.0 copy-start.2
  0.9 0.8 %copy-done.2 = bf16[2,128,128]{2,1,0:T(8,128)(2,1)S(1)} copy-done((bf16[2,128,128]{2,1,0:T(8,128)(2,1)S(1)}, bf16[2,128,128]{2,1,0:T(8,128)(2,1)}, u32[]{:S(2)}) %copy-start.2) | copy-done | bytes 65560
  1.8 0.0 copy-start.3
  1.8 0.7 %copy-done.3 = s32[1,16,29]{2,1,0:T(8,128)S(1)} copy-done((s32[1,16,29]{2,1,0:T(8,128)S(1)}, s32[1,16,29]{2,1,0:T(8,128)}, u32[]{:S(2)}) %copy-start.3) | copy-done | bytes 1880
  2.5 0.0 copy-start
  2.5 60.2 %shard_map.55 = (bf16[16,59392]{1,0:T(8,128)(2,1)S(1)}, f32[1,128]{1,0:T(1,128)S(1)}) custom-call(bf16[2048,3712]{1,0:T(8,128)(2,1)} %bitcast.7, s32[29,16,32]{2,1,0:T(8,128)S(1)} %bitcast.5, s32[16,29]{1,0:T(8,128)S(1)} %bitcast.6, bf16[2,128,128]{2,1,0:T(8,128)(2,1)S(1)} %copy-done.2), custom_call_target="tpu_custom_call" | custom-call | tf_op jit(solution)/shard_map/pallas_call | solution.py:295
  62.7 0.0 copy-done
  62.7 2.1 %shard_map.56 = f32[2,8,59392]{2,1,0:T(8,128)} custom-call(f32[2,8,59392]{2,1,0:T(8,128)S(1)} %copy-done, bf16[16,59392]{1,0:T(8,128)(2,1)S(1)} %get-tuple-element.7.update, f32[1,128]{1,0:T(1,128)S(1)} %get-tuple-element.8.energy), custom_call_target="tpu_custom_call" | custom-call | tf_op jit(solution)/shard_map/pallas_call | solution.py:334
Async XLA Ops:
  0.0 0.9 %copy-start.1 = (s32[1,16,29,32]{3,1,2,0:T(8,128)S(1)}, s32[1,16,29,32]{3,1,2,0:T(8,128)}, u32[]{:S(2)}) copy-start(s32[1,16,29,32]{3,1,2,0:T(8,128)} %param.6) | copy-start | bytes 178180
  0.9 0.8 %copy-start.2 = (bf16[2,128,128]{2,1,0:T(8,128)(2,1)S(1)}, bf16[2,128,128]{2,1,0:T(8,128)(2,1)}, u32[]{:S(2)}) copy-start(bf16[2,128,128]{2,1,0:T(8,128)(2,1)} %constant.7.tables) | copy-start | bytes 196612
  1.8 0.7 %copy-start.3 = (s32[1,16,29]{2,1,0:T(8,128)S(1)}, s32[1,16,29]{2,1,0:T(8,128)}, u32[]{:S(2)}) copy-start(s32[1,16,29]{2,1,0:T(8,128)} %param.7) | copy-start | bytes 5572
  2.5 60.2 %copy-start = (f32[2,8,59392]{2,1,0:T(8,128)S(1)}, f32[2,8,59392]{2,1,0:T(8,128)}, u32[]{:S(2)}) copy-start(f32[2,8,59392]{2,1,0:T(8,128)} %momentum.1) | copy-start | bytes 11403268

commit v4 on v3

--- a/solution.py
+++ b/solution.py
@@ -33,10 +33,10 @@
 
 
 def exchange_kernel(
-    cols, grads, keep_rows, keep_counts, tables, update, energy_out,
+    cols, grads, keep_rows, keep_counts, tables, momentum, update, energy_out, momentum_near,
     x_buf, send_buf, recv_buf, upd_buf, rows_buf, counts_buf, tables_buf,
     lab_wide, lab_mine, lab_send, lab_recv, lab_own, energy, energy_row, energy_a, energy_b,
-    x_sem, in_sem, blk_recv, blk_send, lab_sem, upd_sem, en_sem, ready,
+    x_sem, in_sem, blk_recv, blk_send, lab_sem, upd_sem, en_sem, near_sem, ready,
 ):
     shard = lax.axis_index("shard")
     rep = lax.axis_index("rep")
@@ -58,6 +58,7 @@
         pltpu.make_async_copy(keep_counts, counts_buf, in_sem.at[1]),
         pltpu.make_async_copy(tables, tables_buf, in_sem.at[2]),
     ]
+    near_copy = pltpu.make_async_copy(momentum, momentum_near, near_sem.at[0])
     barrier = pltpu.get_barrier_semaphore()
     for peer in rep_peers:
         pl.semaphore_signal(barrier, inc=1, device_id=(shard, peer), device_id_type=MESH)
@@ -66,8 +67,6 @@
     for copy in small:
         copy.start()
     x_copy(0).start()
-    for k in range(1, len(CHUNKS)):
-        x_copy(k).start()
 
     energy[...] = jnp.zeros_like(energy)
     for copy in small:
@@ -98,6 +97,7 @@
 
     lab_mine[...] = jnp.zeros_like(lab_mine)
     own_rows(0, 1)
+    x_copy(1).start()
 
     def lab_copy(peer):
         return pltpu.make_async_remote_copy(
@@ -112,6 +112,8 @@
 
     def encode(k):
         x_copy(k).wait()
+        if k + 2 < len(CHUNKS):
+            x_copy(k + 2).start()
         pair = min(PAIR, CHUNKS[k])
 
         def columns(step, carry):
@@ -205,12 +207,12 @@
 
     def send_energy():
         energy_row[0] = jnp.sum(energy[...], axis=0, keepdims=True)
-        energy_a[shard] = energy_row[0]
-        for peer in shard_peers:
+        energy_b[rep] = energy_row[0]
+        for peer in rep_peers:
             pltpu.make_async_remote_copy(
-                src_ref=energy_row.at[0], dst_ref=energy_a.at[shard],
-                send_sem=en_sem.at[0], recv_sem=en_sem.at[1],
-                device_id=(peer, rep), device_id_type=MESH).start()
+                src_ref=energy_row.at[0], dst_ref=energy_b.at[rep],
+                send_sem=en_sem.at[2], recv_sem=en_sem.at[3],
+                device_id=(shard, peer), device_id_type=MESH).start()
 
     last = len(CHUNKS)
     encode(0)
@@ -234,6 +236,8 @@
             send_blocks(k + AHEAD)
         if k == 0:
             own_labels()
+        if k == 1:
+            near_copy.start()
         decode(k, send_energy if k == last - 1 else None)
         if k == 0:
             pl.semaphore_wait(ready, len(along_z))
@@ -241,25 +245,26 @@
 
     sent = send_buf.at[pl.ds(0, REPS - 1)]
     pltpu.make_async_copy(sent, sent, blk_send.at[0]).wait()
+    near_copy.wait()
+    over_rep = energy_b.at[pl.ds(0, REPS - 1)]
+    pltpu.make_async_copy(over_rep, over_rep, en_sem.at[3]).wait()
+    energy_row[1] = jnp.sum(energy_b[...], axis=0)
+    energy_a[shard] = energy_row[1]
+    for peer in shard_peers:
+        pltpu.make_async_remote_copy(
+            src_ref=energy_row.at[1], dst_ref=energy_a.at[shard],
+            send_sem=en_sem.at[0], recv_sem=en_sem.at[1],
+            device_id=(peer, rep), device_id_type=MESH).start()
     sent = lab_recv.at[pl.ds(0, REPS - 1)]
     pltpu.make_async_copy(sent, sent, lab_sem.at[0]).wait()
-    others = energy_a.at[pl.ds(0, SHARDS - 1)]
-    pltpu.make_async_copy(others, others, en_sem.at[1]).wait()
-    energy_row[1] = jnp.sum(energy_a[...], axis=0)
-    energy_b[rep] = energy_row[1]
-    for peer in rep_peers:
-        pltpu.make_async_remote_copy(
-            src_ref=energy_row.at[1], dst_ref=energy_b.at[rep],
-            send_sem=en_sem.at[2], recv_sem=en_sem.at[3],
-            device_id=(shard, peer), device_id_type=MESH).start()
-    pltpu.make_async_copy(others, others, en_sem.at[0]).wait()
+    pltpu.make_async_copy(over_rep, over_rep, en_sem.at[2]).wait()
     sent = upd_buf.at[pl.ds(0, SHARDS - 1)]
     pltpu.make_async_copy(sent, sent, upd_sem.at[0]).wait()
     pltpu.make_async_copy(upd_buf, upd_buf, upd_sem.at[1]).wait()
-    others = energy_b.at[pl.ds(0, REPS - 1)]
-    pltpu.make_async_copy(others, others, en_sem.at[3]).wait()
-    energy_out[...] = jnp.sum(energy_b[...], axis=0)
-    pltpu.make_async_copy(others, others, en_sem.at[2]).wait()
+    over_shard = energy_a.at[pl.ds(0, SHARDS - 1)]
+    pltpu.make_async_copy(over_shard, over_shard, en_sem.at[1]).wait()
+    energy_out[...] = jnp.sum(energy_a[...], axis=0)
+    pltpu.make_async_copy(over_shard, over_shard, en_sem.at[0]).wait()
 
 
 def step_kernel(limit, momentum, update, energy, out, out_buf, sems):
@@ -292,14 +297,15 @@
     anywhere = pl.BlockSpec(memory_space=pl.ANY)
     block = (REPS, cols, OWNED * KMAX, TILE)
     part = OWNED * TILE // SHARDS
-    update, energy = pl.pallas_call(
+    update, energy, momentum_near = pl.pallas_call(
         functools.partial(exchange_kernel, cols),
         out_shape=(
             jax.ShapeDtypeStruct((part, full), jnp.bfloat16),
             jax.ShapeDtypeStruct((1, TILE), jnp.float32),
+            jax.ShapeDtypeStruct(momentum.shape, jnp.float32),
         ),
-        in_specs=[pl.BlockSpec(memory_space=pltpu.HBM)] * 4,
-        out_specs=(anywhere, vmem),
+        in_specs=[pl.BlockSpec(memory_space=pltpu.HBM)] * 5,
+        out_specs=(anywhere, vmem, anywhere),
         scratch_shapes=[
             pltpu.VMEM((all_rows, width), jnp.bfloat16),
             pltpu.VMEM(block, jnp.bfloat16),
@@ -308,7 +314,7 @@
             pltpu.VMEM((cols, ROW_TILES, KMAX), jnp.int32),
             pltpu.VMEM((ROW_TILES, cols), jnp.int32),
             pltpu.VMEM((2, TILE, TILE), jnp.bfloat16),
-            pltpu.VMEM((cols * ROW_TILES, TILE), jnp.int32),
+            pltpu.VMEM(((cols + 1) * ROW_TILES, TILE), jnp.int32),
             pltpu.VMEM((4, cols_pad, TILE), jnp.int32),
             pltpu.VMEM((REPS, cols_pad // 2, TILE), jnp.bfloat16),
             pltpu.VMEM((REPS, cols_pad // 2, TILE), jnp.bfloat16),
@@ -324,11 +330,13 @@
             pltpu.SemaphoreType.DMA((2,)),
             pltpu.SemaphoreType.DMA((2,)),
             pltpu.SemaphoreType.DMA((4,)),
+            pltpu.SemaphoreType.DMA((1,)),
             pltpu.SemaphoreType.REGULAR,
         ],
         compiler_params=pltpu.CompilerParams(
             collective_id=0, has_side_effects=True, vmem_limit_bytes=48 * 1024 * 1024),
-    )(gradients[0], jnp.transpose(keep_rows[0], (1, 0, 2)), keep_counts[0], tables)
+    )(*[pltpu.with_memory_space_constraint(v, pltpu.HBM) for v in (
+        gradients[0], jnp.transpose(keep_rows[0], (1, 0, 2)), keep_counts[0], tables, momentum)])
 
     limit = math.sqrt(all_rows * full)
     return pl.pallas_call(
@@ -338,7 +346,7 @@
         out_specs=anywhere,
         scratch_shapes=[pltpu.VMEM(momentum.shape, jnp.float32), pltpu.SemaphoreType.DMA((8,))],
         compiler_params=pltpu.CompilerParams(vmem_limit_bytes=16 * 1024 * 1024),
-    )(momentum, update, energy)
+    )(momentum_near, update, energy)
 
 
 def solution(mesh):

time: 65 us -> 61.6 us (0.948)
  local copies, waits for them, and re-layouts: 2.48 us -> 0 us
  Pallas kernels: 62.3 us -> 61.5 us
    unnamed x8 -> x0, local copies, waits for them, and re-layouts: 2.48 us -> none
    pallas_call x1, Pallas kernels: 60.2 us -> 59.3 us  [body(): pl.pallas_call(functools.partial(exchange_kernel, cols), out_shape=(jax.S...]
where the time goes in v4:
time: 61.6 us; the launch traced here: 61.5 us
  Pallas kernels  61.5 us (100%)
    pallas_call x1, Pallas kernels, body(): pl.pallas_call(functools.partial(exchange_kernel, cols), out_shape=(jax.S...  59.3 us
    pallas_call x1, Pallas kernels, body(): pl.pallas_call(functools.partial(step_kernel, limit), out_shape=jax.Shape...  2.15 us

profile of v4, /device:TPU:1, one launch (start us, length us, event | category | flops | bytes accessed | tf_op | source)
XLA Modules:
  0.0 61.5 jit_solution(1849284697059835821)
XLA Ops:
  0.0 59.3 %shard_map.55 = (bf16[16,59392]{1,0:T(8,128)(2,1)S(1)}, f32[1,128]{1,0:T(1,128)S(1)}, f32[2,8,59392]{2,1,0:T(8,128)S(1)}) custom-call(bf16[2048,3712]{1,0:T(8,128)(2,1)} %bitcast.5, s32[29,16,32]{2,1,0:T(8,128)} %bitcast.6, s32[16,29]{1,0:T(8,128)} %bitcast.7, bf16[2,128,128]{2,1,0:T(8,128)(2,1)} %constant.7.tables, f32[2,8,59392]{2,1,0:T(8,128)} %momentum.1), custom_call_target="tpu_custom_call" | custom-call | tf_op jit(solution)/shard_map/pallas_call | solution.py:300
  59.3 2.1 %shard_map.56 = f32[2,8,59392]{2,1,0:T(8,128)} custom-call(f32[2,8,59392]{2,1,0:T(8,128)S(1)} %get-tuple-element.8.momentum, bf16[16,59392]{1,0:T(8,128)(2,1)S(1)} %get-tuple-element.9.update, f32[1,128]{1,0:T(1,128)S(1)} %get-tuple-element.10.energy), custom_call_target="tpu_custom_call" | custom-call | tf_op jit(solution)/shard_map/pallas_call | solution.py:342

commit v5 on v4

--- a/solution.py
+++ b/solution.py
@@ -45,7 +45,7 @@
                  for y in (2, 1, 3, 0) for core in (0, 1) if y or core]
     hops = sorted(((z, x) for z in range(4) for x in range(4) if z or x), key=lambda p: -(2 - abs(p[0] - 2)) - (2 - abs(p[1] - 2)))
     ring = [lax.rem(shard // 4 + z, 4) * 4 + lax.rem(shard + x, 4) for z, x in hops]
-    shard_peers = [j + (j >= shard).astype(jnp.int32) for j in range(SHARDS - 1)]
+    shard_peers = ring
     near = [peer for peer, (z, x) in zip(ring, hops) if not (z and x)]
     along_z = [peer for peer, (z, x) in zip(ring, hops) if not x]
 
@@ -161,21 +161,23 @@
                         total = jnp.where(slot == i, moved, total)
                     lab_own[q, group, part * half:(part + 1) * half] = total.astype(jnp.int32)
 
+    def places(column, q):
+        return jnp.concatenate([hits(lab_own[q, half, pl.ds(column, 1), :]) for half in range(2)], axis=1)
+
     def decode(k, summed_up=None):
         span = pl.ds(starts[k], CHUNKS[k])
+        pair = min(PAIR, CHUNKS[k])
+        ready_places = [places(starts[k] + i, q) for i in range(pair) for q in range(OWNED)] if CHUNKS[k] == pair else None
         pltpu.make_async_copy(recv_buf.at[:, span], recv_buf.at[:, span], blk_recv.at[k]).wait()
-
-        pair = min(PAIR, CHUNKS[k])
 
         def columns(step, carry):
             first = starts[k] + step * pair
             sums = []
             for i in range(pair):
                 for q in range(OWNED):
-                    places = jnp.concatenate(
-                        [hits(lab_own[q, half, pl.ds(first + i, 1), :]) for half in range(2)], axis=1)
+                    where = ready_places[i * OWNED + q] if ready_places else places(first + i, q)
                     block = recv_buf[:, first + i, q * KMAX:(q + 1) * KMAX, :].reshape(REPS * KMAX, TILE)
-                    sums.append(dot(places, block))
+                    sums.append(dot(where, block))
             squares = sum(jnp.sum((v * v).reshape(TILE // 8, 8, TILE), axis=0) for v in sums)
             energy[...] += squares
             if summed_up is not None:

time: 61.6 us -> 61.6 us (level)
  no operation moved by 1% of the time
where the time goes in v5:
time: 61.6 us; the launch traced here: 61.5 us
  Pallas kernels  61.5 us (100%)
    pallas_call x1, Pallas kernels, body(): pl.pallas_call(functools.partial(exchange_kernel, cols), out_shape=(jax.S...  59.3 us
    pallas_call x1, Pallas kernels, body(): pl.pallas_call(functools.partial(step_kernel, limit), out_shape=jax.Shape...  2.15 us

profile of v5, /device:TPU:1, one launch (start us, length us, event | category | flops | bytes accessed | tf_op | source)
XLA Modules:
  0.0 61.5 jit_solution(15321319757443240728)
XLA Ops:
  0.0 59.3 %shard_map.55 = (bf16[16,59392]{1,0:T(8,128)(2,1)S(1)}, f32[1,128]{1,0:T(1,128)S(1)}, f32[2,8,59392]{2,1,0:T(8,128)S(1)}) custom-call(bf16[2048,3712]{1,0:T(8,128)(2,1)} %bitcast.5, s32[29,16,32]{2,1,0:T(8,128)} %bitcast.6, s32[16,29]{1,0:T(8,128)} %bitcast.7, bf16[2,128,128]{2,1,0:T(8,128)(2,1)} %constant.7.tables, f32[2,8,59392]{2,1,0:T(8,128)} %momentum.1), custom_call_target="tpu_custom_call" | custom-call | tf_op jit(solution)/shard_map/pallas_call | solution.py:302
  59.3 2.1 %shard_map.56 = f32[2,8,59392]{2,1,0:T(8,128)} custom-call(f32[2,8,59392]{2,1,0:T(8,128)S(1)} %get-tuple-element.8.momentum, bf16[16,59392]{1,0:T(8,128)(2,1)S(1)} %get-tuple-element.9.update, f32[1,128]{1,0:T(1,128)S(1)} %get-tuple-element.10.energy), custom_call_target="tpu_custom_call" | custom-call | tf_op jit(solution)/shard_map/pallas_call | solution.py:344
